TPU v7x, 128 devices: a whole 4x4x4 slice. The times are simulated.
128 devices in a mesh: rep: 16 (over y_hi, z, core), shard: 8 (over y_lo, x).
Axes of the slice: x: 4, y: 4 (y_hi: 2, y_lo: 2; y = y_hi * 2 + y_lo), z: 4, core: 2. Of those that a mesh axis runs over, the one named last changes fastest.
Arguments:
- tokens: bfloat16 [18432, 1088], P(('rep', 'shard')), may hold values from -6 to 6
- cotangent: bfloat16 [18432, 1088], P(('rep', 'shard')), may hold values from -6 to 6
- segments: int32 [18432], P('rep'), may hold values from 0 to 33, as said below
- gain_one: bfloat16 [2, 1088], P(None, 'shard'), may hold values from 0.5 to 1.5
- shift_one: bfloat16 [2, 1088], P(None, 'shard'), may hold values from -3 to 3
- w_qkv: bfloat16 [2, 1088, 3264], P(None, 'shard'), may hold values from -0.25 to 0.25
- bias_qv: bfloat16 [2, 2176], P(None, 'shard'), may hold values from -3 to 3
- w_out: bfloat16 [2, 1088, 1088], P(None, 'shard'), may hold values from -0.5 to 0.5
- bias_out: bfloat16 [2, 1088], P(None, 'shard'), may hold values from -3 to 3
- gain_two: bfloat16 [2, 1088], P(None, 'shard'), may hold values from 0.5 to 1.5
- shift_two: bfloat16 [2, 1088], P(None, 'shard'), may hold values from -3 to 3
- w_up: bfloat16 [2, 1088, 4352], P(None, 'shard'), may hold values from -0.1875 to 0.1875
- bias_up: bfloat16 [2, 4352], P(None, 'shard'), may hold values from -3 to 3
- w_down: bfloat16 [2, 4352, 1088], P(None, 'shard'), may hold values from -0.125 to 0.125
- bias_down: bfloat16 [2, 1088], P(None, 'shard'), may hold values from -3 to 3
Outputs:
- output: bfloat16 [18432, 1088], P(('rep', 'shard'))
- grad_tokens: bfloat16 [18432, 1088], P(('rep', 'shard'))
- grad_gain_one: float32 [2, 1088], P(None, 'shard')
- grad_shift_one: float32 [2, 1088], P(None, 'shard')
- grad_w_qkv: float32 [2, 1088, 3264], P(None, 'shard')
- grad_bias_qv: float32 [2, 2176], P(None, 'shard')
- grad_w_out: float32 [2, 1088, 1088], P(None, 'shard')
- grad_bias_out: float32 [2, 1088], P(None, 'shard')
- grad_gain_two: float32 [2, 1088], P(None, 'shard')
- grad_shift_two: float32 [2, 1088], P(None, 'shard')
- grad_w_up: float32 [2, 1088, 4352], P(None, 'shard')
- grad_bias_up: float32 [2, 4352], P(None, 'shard')
- grad_w_down: float32 [2, 4352, 1088], P(None, 'shard')
- grad_bias_down: float32 [2, 1088], P(None, 'shard')
Inputs may be any that keep to these rules, and one draw needn't show every extreme that they name: `segments`: within each pack of 1152 tokens the sequence numbers start at 0, never fall and rise by at most one from token to token; every pack holds exactly 34 sequences; one holds exactly 1024 tokens and starts among the pack's first 129 positions, after at least one other sequence.
All inputs are finite; a program needn't handle non-finite values.
Results may differ from a plain program's by a relative error of at most 0.028.
Values may be sent and summed in bfloat16 or wider, within the bound.
No kernel may reach another device: no remote copies, remote signals or barrier semaphores. Data moves between devices by JAX's collectives and lax.ppermute only.
A program may use at most 256 MiB of HBM per device.

v0:
```python
import math

import jax
import jax.numpy as jnp
from jax import lax
from jax.sharding import PartitionSpec as P

HEADS = 17
HEAD_DIM = 64
LAYERS = 2


epsilon = 1e-05


def norm_rows(inputs, gain, shift):
    average = jnp.mean(inputs, axis=-1, keepdims=True)
    centered = inputs - average
    variance = jnp.mean(centered * centered, axis=-1, keepdims=True)
    return centered * lax.rsqrt(variance + epsilon) * gain + shift


def gelu_tanh(inputs):
    return jax.nn.gelu(inputs, approximate=True)


def fetch_forward(pieces):
    return (
        lax.all_gather(pieces[0], "shard", axis=0, tiled=True),
        lax.all_gather(pieces[1], "shard", axis=0, tiled=True),
        lax.all_gather(pieces[2], "shard", axis=0, tiled=True),
        lax.all_gather(pieces[3], "shard", axis=0, tiled=True),
        lax.all_gather(pieces[4], "shard", axis=0, tiled=True),
        lax.all_gather(pieces[5], "shard", axis=0, tiled=True),
        lax.all_gather(pieces[6], "shard", axis=0, tiled=True),
        lax.all_gather(pieces[7], "shard", axis=0, tiled=True),
        lax.all_gather(pieces[8], "shard", axis=0, tiled=True),
        lax.all_gather(pieces[9], "shard", axis=0, tiled=True),
        lax.all_gather(pieces[10], "shard", axis=0, tiled=True),
        lax.all_gather(pieces[11], "shard", axis=0, tiled=True),
    )


def fetch_backward(pieces):
    return (
        lax.all_gather(pieces[0], "shard", axis=0, tiled=True),
        lax.all_gather(pieces[1], "shard", axis=0, tiled=True),
        lax.all_gather(pieces[2], "shard", axis=0, tiled=True),
        lax.all_gather(pieces[3], "shard", axis=0, tiled=True),
        lax.all_gather(pieces[4], "shard", axis=0, tiled=True),
        lax.all_gather(pieces[5], "shard", axis=0, tiled=True),
        lax.all_gather(pieces[6], "shard", axis=0, tiled=True),
        lax.all_gather(pieces[7], "shard", axis=0, tiled=True),
        lax.all_gather(pieces[8], "shard", axis=0, tiled=True),
        lax.all_gather(pieces[9], "shard", axis=0, tiled=True),
        lax.all_gather(pieces[10], "shard", axis=0, tiled=True),
        lax.all_gather(pieces[11], "shard", axis=0, tiled=True),
    )


def owner_sums(terms):
    return (
        lax.psum_scatter(
            terms[0].astype(jnp.bfloat16), "shard", scatter_dimension=0, tiled=True
        ).astype(jnp.float32),
        lax.psum_scatter(
            terms[1].astype(jnp.bfloat16), "shard", scatter_dimension=0, tiled=True
        ).astype(jnp.float32),
        lax.psum_scatter(
            terms[2].astype(jnp.bfloat16), "shard", scatter_dimension=0, tiled=True
        ).astype(jnp.float32),
        lax.psum_scatter(
            terms[3].astype(jnp.bfloat16), "shard", scatter_dimension=0, tiled=True
        ).astype(jnp.float32),
        lax.psum_scatter(
            terms[4].astype(jnp.bfloat16), "shard", scatter_dimension=0, tiled=True
        ).astype(jnp.float32),
        lax.psum_scatter(
            terms[5].astype(jnp.bfloat16), "shard", scatter_dimension=0, tiled=True
        ).astype(jnp.float32),
        lax.psum_scatter(
            terms[6].astype(jnp.bfloat16), "shard", scatter_dimension=0, tiled=True
        ).astype(jnp.float32),
        lax.psum_scatter(
            terms[7].astype(jnp.bfloat16), "shard", scatter_dimension=0, tiled=True
        ).astype(jnp.float32),
        lax.psum_scatter(
            terms[8].astype(jnp.bfloat16), "shard", scatter_dimension=0, tiled=True
        ).astype(jnp.float32),
        lax.psum_scatter(
            terms[9].astype(jnp.bfloat16), "shard", scatter_dimension=0, tiled=True
        ).astype(jnp.float32),
        lax.psum_scatter(
            terms[10].astype(jnp.bfloat16), "shard", scatter_dimension=0, tiled=True
        ).astype(jnp.float32),
        lax.psum_scatter(
            terms[11].astype(jnp.bfloat16), "shard", scatter_dimension=0, tiled=True
        ).astype(jnp.float32),
    )


def replica_layer_sum(terms):
    return (
        lax.psum(terms[0].astype(jnp.bfloat16), "rep").astype(jnp.float32),
        lax.psum(terms[1].astype(jnp.bfloat16), "rep").astype(jnp.float32),
        lax.psum(terms[2].astype(jnp.bfloat16), "rep").astype(jnp.float32),
        lax.psum(terms[3].astype(jnp.bfloat16), "rep").astype(jnp.float32),
        lax.psum(terms[4].astype(jnp.bfloat16), "rep").astype(jnp.float32),
        lax.psum(terms[5].astype(jnp.bfloat16), "rep").astype(jnp.float32),
        lax.psum(terms[6].astype(jnp.bfloat16), "rep").astype(jnp.float32),
        lax.psum(terms[7].astype(jnp.bfloat16), "rep").astype(jnp.float32),
        lax.psum(terms[8].astype(jnp.bfloat16), "rep").astype(jnp.float32),
        lax.psum(terms[9].astype(jnp.bfloat16), "rep").astype(jnp.float32),
        lax.psum(terms[10].astype(jnp.bfloat16), "rep").astype(jnp.float32),
        lax.psum(terms[11].astype(jnp.bfloat16), "rep").astype(jnp.float32),
    )


def score_block(heads_q, heads_k, allowed, score_scale):
    scores = (
        jnp.einsum("thd,shd->hts", heads_q, heads_k, preferred_element_type=jnp.float32)
        * score_scale
    )
    return jnp.where(allowed[None], scores, -1e30)


def forward_layer(stream, gathered, allowed, score_scale):
    (
        gain_a,
        shift_a,
        mix_weight,
        mix_bias,
        out_weight,
        out_bias,
        gain_b,
        shift_b,
        up_weight,
        up_bias,
        down_weight,
        down_bias,
    ) = gathered
    row_count, feature_count = stream.shape
    normed = norm_rows(stream, gain_a.astype(jnp.float32), shift_a.astype(jnp.float32)).astype(
        jnp.bfloat16
    )
    mixed = jnp.dot(normed, mix_weight, preferred_element_type=jnp.float32)
    bias_full = mix_bias.astype(jnp.float32)
    queries = (mixed[:, :feature_count] + bias_full[:feature_count]).astype(jnp.bfloat16)
    key_rows = mixed[:, feature_count : 2 * feature_count].astype(jnp.bfloat16)
    values = (mixed[:, 2 * feature_count :] + bias_full[feature_count:]).astype(jnp.bfloat16)
    keys_all, values_all = (
        lax.all_gather(key_rows, "shard", axis=0, tiled=True),
        lax.all_gather(values, "shard", axis=0, tiled=True),
    )
    heads_q = queries.reshape(row_count, HEADS, HEAD_DIM)
    heads_k = keys_all.reshape(-1, HEADS, HEAD_DIM)
    heads_v = values_all.reshape(-1, HEADS, HEAD_DIM)
    scores = score_block(heads_q, heads_k, allowed, score_scale)
    highest = jnp.max(scores, axis=-1, keepdims=True)
    exponent = jnp.exp(scores - highest)
    row_total = jnp.sum(exponent, axis=-1, keepdims=True)
    probability = exponent / row_total
    log_total = highest + jnp.log(row_total)
    weights = probability.astype(jnp.bfloat16)
    attended = jnp.einsum("hts,shd->thd", weights, heads_v, preferred_element_type=jnp.float32)
    attended = attended.reshape(row_count, feature_count).astype(jnp.bfloat16)
    stream_mid = (
        stream
        + jnp.dot(attended, out_weight, preferred_element_type=jnp.float32)
        + out_bias.astype(jnp.float32)
    )
    normed_b = norm_rows(
        stream_mid, gain_b.astype(jnp.float32), shift_b.astype(jnp.float32)
    ).astype(jnp.bfloat16)
    up_value = jnp.dot(normed_b, up_weight, preferred_element_type=jnp.float32) + up_bias.astype(
        jnp.float32
    )
    active = gelu_tanh(up_value).astype(jnp.bfloat16)
    result = (
        stream_mid
        + jnp.dot(active, down_weight, preferred_element_type=jnp.float32)
        + down_bias.astype(jnp.float32)
    )
    retained = (
        stream,
        normed,
        heads_q,
        heads_k,
        heads_v,
        log_total,
        attended,
        stream_mid,
        normed_b,
        up_value,
        active,
    )
    return (retained, result)


def backward_layer(gradient, gathered, retained, allowed, score_scale):
    (
        gain_a,
        shift_a,
        mix_weight,
        mix_bias,
        out_weight,
        out_bias,
        gain_b,
        shift_b,
        up_weight,
        up_bias,
        down_weight,
        down_bias,
    ) = gathered
    (
        stream,
        normed,
        heads_q,
        heads_k,
        heads_v,
        log_total,
        attended,
        stream_mid,
        normed_b,
        up_value,
        active,
    ) = retained
    row_count, feature_count = stream.shape
    grad_branch = gradient.astype(jnp.bfloat16)
    grad_active = jnp.einsum(
        "td,fd->tf", grad_branch, down_weight, preferred_element_type=jnp.float32
    )
    unused_gelu, gelu_pull = jax.vjp(gelu_tanh, up_value)
    grad_up = gelu_pull(grad_active)[0].astype(jnp.bfloat16)
    grad_normed_b = jnp.einsum("tf,df->td", grad_up, up_weight, preferred_element_type=jnp.float32)
    unused_norm_b, norm_pull_b = jax.vjp(
        norm_rows, stream_mid, gain_b.astype(jnp.float32), shift_b.astype(jnp.float32)
    )
    grad_mid_norm, grad_gain_b, grad_shift_b = norm_pull_b(grad_normed_b)
    grad_mid = gradient + grad_mid_norm
    grad_attn = grad_mid.astype(jnp.bfloat16)
    grad_attended = jnp.einsum(
        "te,de->td", grad_attn, out_weight, preferred_element_type=jnp.float32
    ).astype(jnp.bfloat16)
    grad_heads_o = grad_attended.reshape(row_count, HEADS, HEAD_DIM)
    scores = score_block(heads_q, heads_k, allowed, score_scale)
    probability = jnp.exp(scores - log_total)
    weights = probability.astype(jnp.bfloat16)
    grad_prob = jnp.einsum(
        "thd,shd->hts", grad_heads_o, heads_v, preferred_element_type=jnp.float32
    )
    inner_sum = jnp.sum(grad_prob * probability, axis=-1, keepdims=True)
    grad_scores = (probability * (grad_prob - inner_sum)).astype(jnp.bfloat16)
    grad_queries = (
        jnp.einsum("hts,shd->thd", grad_scores, heads_k, preferred_element_type=jnp.float32)
        * score_scale
    )
    grad_keys_part = (
        jnp.einsum("hts,thd->shd", grad_scores, heads_q, preferred_element_type=jnp.float32)
        * score_scale
    )
    grad_values_part = jnp.einsum(
        "hts,thd->shd", weights, grad_heads_o, preferred_element_type=jnp.float32
    )
    grad_keys, grad_values = (
        lax.psum_scatter(
            grad_keys_part.reshape(-1, feature_count).astype(jnp.bfloat16),
            "shard",
            scatter_dimension=0,
            tiled=True,
        ).astype(jnp.float32),
        lax.psum_scatter(
            grad_values_part.reshape(-1, feature_count).astype(jnp.bfloat16),
            "shard",
            scatter_dimension=0,
            tiled=True,
        ).astype(jnp.float32),
    )
    grad_queries = grad_queries.reshape(row_count, feature_count).astype(jnp.bfloat16)
    grad_keys = grad_keys.astype(jnp.bfloat16)
    grad_values = grad_values.astype(jnp.bfloat16)
    grad_mixed = jnp.concatenate([grad_queries, grad_keys, grad_values], axis=1)
    grad_normed = jnp.einsum(
        "te,de->td", grad_mixed, mix_weight, preferred_element_type=jnp.float32
    )
    unused_norm_a, norm_pull_a = jax.vjp(
        norm_rows, stream, gain_a.astype(jnp.float32), shift_a.astype(jnp.float32)
    )
    grad_in_norm, grad_gain_a, grad_shift_a = norm_pull_a(grad_normed)
    grad_in = grad_mid + grad_in_norm
    grad_down_w = jnp.einsum("tf,td->fd", active, grad_branch, preferred_element_type=jnp.float32)
    grad_down_b = jnp.sum(grad_branch.astype(jnp.float32), axis=0)
    grad_up_w = jnp.einsum("td,tf->df", normed_b, grad_up, preferred_element_type=jnp.float32)
    grad_up_b = jnp.sum(grad_up.astype(jnp.float32), axis=0)
    grad_out_w = jnp.einsum("td,te->de", attended, grad_attn, preferred_element_type=jnp.float32)
    grad_out_b = jnp.sum(grad_attn.astype(jnp.float32), axis=0)
    grad_mix_w = jnp.einsum("td,te->de", normed, grad_mixed, preferred_element_type=jnp.float32)
    grad_mix_b = jnp.concatenate(
        [
            jnp.sum(grad_queries.astype(jnp.float32), axis=0),
            jnp.sum(grad_values.astype(jnp.float32), axis=0),
        ]
    )
    gradients = (
        grad_gain_a,
        grad_shift_a,
        grad_mix_w,
        grad_mix_b,
        grad_out_w,
        grad_out_b,
        grad_gain_b,
        grad_shift_b,
        grad_up_w,
        grad_up_b,
        grad_down_w,
        grad_down_b,
    )
    owned = owner_sums(gradients)
    return (grad_in, owned)


def body(
    tokens,
    cotangent,
    segments,
    gain_one,
    shift_one,
    w_qkv,
    bias_qv,
    w_out,
    bias_out,
    gain_two,
    shift_two,
    w_up,
    bias_up,
    w_down,
    bias_down,
):
    shards = (
        gain_one,
        shift_one,
        w_qkv,
        bias_qv,
        w_out,
        bias_out,
        gain_two,
        shift_two,
        w_up,
        bias_up,
        w_down,
        bias_down,
    )
    row_count = tokens.shape[0]
    member = lax.axis_index("shard")
    positions = member * row_count + jnp.arange(row_count, dtype=jnp.int32)
    columns = jnp.arange(segments.shape[0], dtype=jnp.int32)
    own_segments = lax.dynamic_slice_in_dim(segments, member * row_count, row_count)
    allowed = (own_segments[:, None] == segments[None, :]) & (
        columns[None, :] <= positions[:, None]
    )
    score_scale = 1.0 / math.sqrt(HEAD_DIM)
    stream = tokens.astype(jnp.float32)
    stored = []
    for depth in range(LAYERS):
        gathered = fetch_forward(tuple((shard_piece[depth] for shard_piece in shards)))
        retained, stream = forward_layer(stream, gathered, allowed, score_scale)
        stored.append((None, retained))
    output = stream.astype(jnp.bfloat16)
    gradient = cotangent.astype(jnp.float32)
    owned = [None] * LAYERS
    for depth in reversed(range(LAYERS)):
        gathered = fetch_backward(tuple((shard_piece[depth] for shard_piece in shards)))
        gradient, layer_owned = backward_layer(
            gradient, gathered, stored[depth][1], allowed, score_scale
        )
        layer_owned = replica_layer_sum(layer_owned)
        owned[depth] = layer_owned
    stacked = tuple(
        (jnp.stack([owned[depth][position] for depth in range(LAYERS)]) for position in range(12))
    )
    return (
        output,
        gradient.astype(jnp.bfloat16),
        stacked[0],
        stacked[1],
        stacked[2],
        stacked[3],
        stacked[4],
        stacked[5],
        stacked[6],
        stacked[7],
        stacked[8],
        stacked[9],
        stacked[10],
        stacked[11],
    )


def solution(mesh):
    in_specs = (
        P(("rep", "shard"), None),
        P(("rep", "shard"), None),
        P("rep"),
        P(None, "shard"),
        P(None, "shard"),
        P(None, "shard", None),
        P(None, "shard"),
        P(None, "shard", None),
        P(None, "shard"),
        P(None, "shard"),
        P(None, "shard"),
        P(None, "shard", None),
        P(None, "shard"),
        P(None, "shard", None),
        P(None, "shard"),
    )
    out_specs = (
        P(("rep", "shard"), None),
        P(("rep", "shard"), None),
        P(None, "shard"),
        P(None, "shard"),
        P(None, "shard", None),
        P(None, "shard"),
        P(None, "shard", None),
        P(None, "shard"),
        P(None, "shard"),
        P(None, "shard"),
        P(None, "shard", None),
        P(None, "shard"),
        P(None, "shard", None),
        P(None, "shard"),
    )
    return jax.shard_map(body, mesh=mesh, in_specs=in_specs, out_specs=out_specs, check_vma=False)
```

profile of v0, /device:TPU:0, one launch (start us, length us, event | category | flops | bytes accessed | tf_op | source)
XLA Modules:
  0.0 1989.7 jit_solution(7410420189909433046)
XLA Ops:
  17.1 37.8 %all-reduce.37 = (bf16[1088]{0:T(1024)(128)(2,1)S(1)}, bf16[1088]{0:T(1024)(128)(2,1)S(1)}, bf16[2176]{0:T(1024)(128)(2,1)S(1)}, bf16[1088]{0:T(1024)(128)(2,1)S...) all-reduce(bf16[1088]{0:T(1024)(128)(2,1)S(1)} %dynamic-update-slic, ...), channel_id=3, replica_groups=mesh['rep'=16,'shard'=8] {'shard'}, use_global_device_ids=true, to_apply=%add.1 | all-reduce | flops 25024 | bytes 100096
  55.5 40.2 %all-gather.45.cloned.1.call-done = bf16[1,1088,3264]{2,1,0:T(8,128)(2,1)} async-done(((bf16[1,136,3264]{2,1,0:T(8,128)(2,1)}), bf16[1,1088,3264]{2,1,0:T(8,128)(2,1)}) %all-gather.45.cloned.1.call-update) | async-done | bytes 7102480 | tf_op jit(solution)/shard_map/all_gather | solution.py:31
  110.7 31.5 %all-gather.37.cloned.1.call-done = bf16[1152,1088]{1,0:T(8,128)(2,1)} async-done(((bf16[144,1088]{1,0:T(8,128)(2,1)}), bf16[1152,1088]{1,0:T(8,128)(2,1)}) %all-gather.37.cloned.1.call-update) | async-done | bytes 2506768 | tf_op jit(solution)/shard_map/all_gather | solution.py:153
  147.3 38.3 %all-gather.39.cloned.1.call-done = bf16[1152,1088]{1,0:T(8,128)(2,1)} async-done(((bf16[144,1088]{1,0:T(8,128)(2,1)}), bf16[1152,1088]{1,0:T(8,128)(2,1)}) %all-gather.39.cloned.1.call-update) | async-done | bytes 2506768 | tf_op jit(solution)/shard_map/all_gather | solution.py:152
  200.4 28.2 %all-gather.47.cloned.1.call-done = bf16[1,1088,1088]{2,1,0:T(8,128)(2,1)} async-done(((bf16[1,136,1088]{2,1,0:T(8,128)(2,1)}), bf16[1,1088,1088]{2,1,0:T(8,128)(2,1)}) %all-gather.47.cloned.1.call-update) | async-done | bytes 2367504 | tf_op jit(solution)/shard_map/all_gather | solution.py:33
  231.4 101.2 %all-gather.49.cloned.1.call-done = bf16[1,1088,4352]{2,1,0:T(8,128)(2,1)} async-done(((bf16[1,136,4352]{2,1,0:T(8,128)(2,1)}), bf16[1,1088,4352]{2,1,0:T(8,128)(2,1)}) %all-gather.49.cloned.1.call-update) | async-done | bytes 9469968 | tf_op jit(solution)/shard_map/all_gather | solution.py:37
  339.6 101.1 %all-gather.51.cloned.1.call-done = bf16[1,4352,1088]{2,1,0:T(8,128)(2,1)} async-done(((bf16[1,544,1088]{2,1,0:T(8,128)(2,1)}), bf16[1,4352,1088]{2,1,0:T(8,128)(2,1)}) %all-gather.51.cloned.1.call-update) | async-done | bytes 9469968 | tf_op jit(solution)/shard_map/all_gather | solution.py:39
  447.8 74.6 %all-gather.53.cloned.1.call-done = bf16[1,1088,3264]{2,1,0:T(8,128)(2,1)} async-done(((bf16[1,136,3264]{2,1,0:T(8,128)(2,1)}), bf16[1,1088,3264]{2,1,0:T(8,128)(2,1)}) %all-gather.53.cloned.1.call-update) | async-done | bytes 7102480 | tf_op jit(solution)/shard_map/all_gather | solution.py:31
  533.6 36.6 %all-gather.41.cloned.1.call-done = bf16[1152,1088]{1,0:T(8,128)(2,1)} async-done(((bf16[144,1088]{1,0:T(8,128)(2,1)}), bf16[1152,1088]{1,0:T(8,128)(2,1)}) %all-gather.41.cloned.1.call-update) | async-done | bytes 2506768 | tf_op jit(solution)/shard_map/all_gather | solution.py:153
  575.3 38.8 %all-gather.43.cloned.1.call-done = bf16[1152,1088]{1,0:T(8,128)(2,1)} async-done(((bf16[144,1088]{1,0:T(8,128)(2,1)}), bf16[1152,1088]{1,0:T(8,128)(2,1)}) %all-gather.43.cloned.1.call-update) | async-done | bytes 2506768 | tf_op jit(solution)/shard_map/all_gather | solution.py:152
  630.5 27.2 %all-gather.55.cloned.1.call-done = bf16[1,1088,1088]{2,1,0:T(8,128)(2,1)} async-done(((bf16[1,136,1088]{2,1,0:T(8,128)(2,1)}), bf16[1,1088,1088]{2,1,0:T(8,128)(2,1)}) %all-gather.55.cloned.1.call-update) | async-done | bytes 2367504 | tf_op jit(solution)/shard_map/all_gather | solution.py:33
  661.1 99.8 %all-gather.57.cloned.1.call-done = bf16[1,1088,4352]{2,1,0:T(8,128)(2,1)} async-done(((bf16[1,136,4352]{2,1,0:T(8,128)(2,1)}), bf16[1,1088,4352]{2,1,0:T(8,128)(2,1)}) %all-gather.57.cloned.1.call-update) | async-done | bytes 9469968 | tf_op jit(solution)/shard_map/all_gather | solution.py:37
  767.9 101.1 %all-gather.59.cloned.1.call-done = bf16[1,4352,1088]{2,1,0:T(8,128)(2,1)} async-done(((bf16[1,544,1088]{2,1,0:T(8,128)(2,1)}), bf16[1,4352,1088]{2,1,0:T(8,128)(2,1)}) %all-gather.59.cloned.1.call-update) | async-done | bytes 9469968 | tf_op jit(solution)/shard_map/all_gather | solution.py:39
  869.1 8.4 fusion.150
  927.3 14.5 reduce-scatter.41.cloned.1.call-done
  943.8 44.5 %reduce-scatter.39.cloned.1.call-done = bf16[144,1088]{1,0:T(8,128)(2,1)} async-done(((bf16[1152,1088]{1,0:T(8,128)(2,1)}), bf16[144,1088]{1,0:T(8,128)(2,1)}) %reduce-scatter.39.cloned.1.call-update) | async-done | bytes 313360
  999.0 8.1 fusion.151
  1016.7 8.2 fusion.45
  1069.8 9.0 convolution_convert_fusion
  1086.3 8.9 convolution_convert_fusion.1
  1111.6 8.9 reduce-scatter.43.cloned.1.call-done
  1128.5 38.9 %reduce-scatter.49.cloned.1.call-done = bf16[136,1088]{1,0:T(8,128)(2,1)} async-done(((bf16[1088,1088]{1,0:T(8,128)(2,1)}), bf16[136,1088]{1,0:T(8,128)(2,1)}) %reduce-scatter.49.cloned.1.call-update) | async-done | bytes 295952
  1167.4 46.7 %reduce-scatter.47.cloned.1.call-done = bf16[136,1088]{1,0:T(8,128)(2,1)} async-done(((bf16[1088,1088]{1,0:T(8,128)(2,1)}), bf16[136,1088]{1,0:T(8,128)(2,1)}) %reduce-scatter.47.cloned.1.call-update) | async-done | bytes 295952
  1214.1 104.5 %reduce-scatter.33.cloned.1.call-done = bf16[136,4352]{1,0:T(8,128)(2,1)} async-done(((bf16[1088,4352]{1,0:T(8,128)(2,1)}), bf16[136,4352]{1,0:T(8,128)(2,1)}) %reduce-scatter.33.cloned.1.call-update) | async-done | bytes 1183760 | tf_op jit(solution)/shard_map/reduce_scatter | solution.py:87
  1318.6 109.2 %reduce-scatter.37.cloned.1.call-done = bf16[544,1088]{1,0:T(8,128)(2,1)} async-done(((bf16[4352,1088]{1,0:T(8,128)(2,1)}), bf16[544,1088]{1,0:T(8,128)(2,1)}) %reduce-scatter.37.cloned.1.call-update) | async-done | bytes 1183760 | tf_op jit(solution)/shard_map/reduce_scatter | solution.py:93
  1427.8 83.4 %reduce-scatter.29.cloned.1.call-done = bf16[136,3264]{1,0:T(8,128)(2,1)} async-done(((bf16[1088,3264]{1,0:T(8,128)(2,1)}), bf16[136,3264]{1,0:T(8,128)(2,1)}) %reduce-scatter.29.cloned.1.call-update) | async-done | bytes 887824 | tf_op jit(solution)/shard_map/reduce_scatter | solution.py:69
  1511.2 109.5 %reduce-scatter.35.cloned.1.call-done = bf16[544,1088]{1,0:T(8,128)(2,1)} async-done(((bf16[4352,1088]{1,0:T(8,128)(2,1)}), bf16[544,1088]{1,0:T(8,128)(2,1)}) %reduce-scatter.35.cloned.1.call-update) | async-done | bytes 1183760 | tf_op jit(solution)/shard_map/reduce_scatter | solution.py:93
  1620.7 104.6 %reduce-scatter.31.cloned.1.call-done = bf16[136,4352]{1,0:T(8,128)(2,1)} async-done(((bf16[1088,4352]{1,0:T(8,128)(2,1)}), bf16[136,4352]{1,0:T(8,128)(2,1)}) %reduce-scatter.31.cloned.1.call-update) | async-done | bytes 1183760 | tf_op jit(solution)/shard_map/reduce_scatter | solution.py:87
  1725.2 83.4 %reduce-scatter.27.cloned.1.call-done = bf16[136,3264]{1,0:T(8,128)(2,1)} async-done(((bf16[1088,3264]{1,0:T(8,128)(2,1)}), bf16[136,3264]{1,0:T(8,128)(2,1)}) %reduce-scatter.27.cloned.1.call-update) | async-done | bytes 887824 | tf_op jit(solution)/shard_map/reduce_scatter | solution.py:69
  1818.2 33.1 %all-reduce.36 = (bf16[1088]{0:T(1024)(128)(2,1)S(1)}, bf16[1088]{0:T(1024)(128)(2,1)S(1)}, bf16[1088]{0:T(1024)(128)(2,1)S(1)}, bf16[1088]{0:T(1024)(128)(2,1)S...) all-reduce(bf16[1088]{0:T(1024)(128)(2,1)S(1)} %dynamic-update-slic, ...), channel_id=25, replica_groups=mesh['rep'=16,'shard'=8] {'shard'}, use_global_device_ids=true, to_apply=%add.15 | all-reduce | flops 27200 | bytes 108800
  1852.7 65.4 %all-reduce.34 = (bf16[1,136]{1,0:T(2,128)(2,1)S(1)}, bf16[1,136]{1,0:T(2,128)(2,1)S(1)}, bf16[1,136]{1,0:T(2,128)(2,1)S(1)}, bf16[1,136]{1,0:T(2,128)(2,1)S(1)}...) all-reduce(bf16[1,136]{1,0:T(2,128)(2,1)S(1)} %stack.169, ...), channel_id=1, replica_groups=mesh['rep'=16,'shard'=8] {'rep'}, use_global_device_ids=true, to_apply=%region_31.32 | all-reduce | flops 3264 | bytes 13056 | tf_op jit(solution)/shard_map/psum | solution.py:104
  1928.9 43.5 %all-reduce.40.cloned.1.call-done = (bf16[1,136,3264]{2,1,0:T(8,128)(2,1)}, bf16[1,136,3264]{2,1,0:T(8,128)(2,1)}, bf16[1,136,1088]{2,1,0:T(8,128)(2,1)}, bf16[1...) async-done(((bf16[1,136,3264]{2,1,0:T(8,128)(2,1)}, ...) | async-done | bytes 7102480 | tf_op jit(solution)/shard_map/psum | solution.py:106
  (501 shorter events, 281.2 us)
Async XLA Ops:
  7.3 88.4 %all-gather.45.cloned.1.call-start = ((), (), s32[]{:S(2)}) async-start(), calls=%async_computation.22 | async-start | bytes 8146944 | tf_op jit(solution)/shard_map/all_gather | solution.py:31
  10.2 131.9 %all-gather.37.cloned.1.call-start = ((), (), s32[]{:S(2)}) async-start(), calls=%async_computation.12 | async-start | bytes 2985984 | tf_op jit(solution)/shard_map/all_gather | solution.py:153
  101.3 84.2 %all-gather.39.cloned.1.call-start = ((), (), s32[]{:S(2)}) async-start(), calls=%async_computation.13 | async-start | bytes 2985984 | tf_op jit(solution)/shard_map/all_gather | solution.py:152
  102.3 126.4 %all-gather.47.cloned.1.call-start = ((), (), s32[]{:S(2)}) async-start(), calls=%async_computation.23 | async-start | bytes 2820096 | tf_op jit(solution)/shard_map/all_gather | solution.py:33
  103.2 229.3 %all-gather.49.cloned.1.call-start = ((), (), s32[]{:S(2)}) async-start(), calls=%async_computation.24 | async-start | bytes 10653696 | tf_op jit(solution)/shard_map/all_gather | solution.py:37
  106.7 334.1 %all-gather.51.cloned.1.call-start = ((), (), s32[]{:S(2)}) async-start(), calls=%async_computation.25 | async-start | bytes 11280384 | tf_op jit(solution)/shard_map/all_gather | solution.py:39
  108.4 413.9 %all-gather.53.cloned.1.call-start = ((), (), s32[]{:S(2)}) async-start(), calls=%async_computation.26 | async-start | bytes 8146944 | tf_op jit(solution)/shard_map/all_gather | solution.py:31
  109.1 461.0 %all-gather.41.cloned.1.call-start = ((), (), s32[]{:S(2)}) async-start(), calls=%async_computation.14 | async-start | bytes 2985984 | tf_op jit(solution)/shard_map/all_gather | solution.py:153
  109.2 413.1 %copy-start.56 = (f32[1088]{0:T(1024)}, f32[1088]{0:T(1024)S(1)}, u32[]{:S(2)}) copy-start(f32[1088]{0:T(1024)S(1)} %convert_element_type.481) | copy-start | bytes 13060
  109.2 223.3 %copy-start.62 = (f32[1088]{0:T(1024)}, f32[1088]{0:T(1024)S(1)}, u32[]{:S(2)}) copy-start(f32[1088]{0:T(1024)S(1)} %convert_element_type.478) | copy-start | bytes 13060
  109.3 413.1 %copy-start.64 = (f32[1088]{0:T(1024)}, f32[1088]{0:T(1024)S(1)}, u32[]{:S(2)}) copy-start(f32[1088]{0:T(1024)S(1)} %convert_element_type.482) | copy-start | bytes 13060
  529.2 84.9 %all-gather.43.cloned.1.call-start = ((), (), s32[]{:S(2)}) async-start(), calls=%async_computation.15 | async-start | bytes 2985984 | tf_op jit(solution)/shard_map/all_gather | solution.py:152
  531.3 126.4 %all-gather.55.cloned.1.call-start = ((), (), s32[]{:S(2)}) async-start(), calls=%async_computation.27 | async-start | bytes 2820096 | tf_op jit(solution)/shard_map/all_gather | solution.py:33
  531.9 229.0 %all-gather.57.cloned.1.call-start = ((), (), s32[]{:S(2)}) async-start(), calls=%async_computation.28 | async-start | bytes 10653696 | tf_op jit(solution)/shard_map/all_gather | solution.py:37
  532.6 336.4 %all-gather.59.cloned.1.call-start = ((), (), s32[]{:S(2)}) async-start(), calls=%async_computation.29 | async-start | bytes 11280384 | tf_op jit(solution)/shard_map/all_gather | solution.py:39
  533.2 408.6 %reduce-scatter.41.cloned.1.call-start = ((), (), s32[]{:S(2)}) async-start(), calls=%async_computation.31 | async-start | bytes 2985984
  533.3 348.6 %copy-start.53 = (f32[1088]{0:T(1024)}, f32[1088]{0:T(1024)S(1)}, u32[]{:S(2)}) copy-start(f32[1088]{0:T(1024)S(1)} %convert_element_type.485) | copy-start | bytes 13060
  533.3 227.6 %copy-start.66 = (f32[1088]{0:T(1024)}, f32[1088]{0:T(1024)S(1)}, u32[]{:S(2)}) copy-start(f32[1088]{0:T(1024)S(1)} %convert_element_type.486) | copy-start | bytes 13060
  660.2 221.6 %copy-start.72 = (f32[144]{0:T(256)}, f32[144]{0:T(256)S(1)}, u32[]{:S(2)}) copy-start(f32[144]{0:T(256)S(1)} %broadcast_multiply_fusion) | copy-start | bytes 1732
  660.5 221.4 %copy-start.78 = (f32[144]{0:T(256)}, f32[144]{0:T(256)S(1)}, u32[]{:S(2)}) copy-start(f32[144]{0:T(256)S(1)} %fusion.120) | copy-start | bytes 1732
  898.0 90.2 %reduce-scatter.39.cloned.1.call-start = ((), (), s32[]{:S(2)}) async-start(), calls=%async_computation.30 | async-start | bytes 2985984
  920.7 189.7 %reduce-scatter.45.cloned.1.call-start = ((), (), s32[]{:S(2)}) async-start(), calls=%async_computation.33 | async-start | bytes 2985984
  1030.2 90.4 %reduce-scatter.43.cloned.1.call-start = ((), (), s32[]{:S(2)}) async-start(), calls=%async_computation.32 | async-start | bytes 2985984
  1053.2 114.2 %reduce-scatter.49.cloned.1.call-start = ((), (), s32[]{:S(2)}) async-start(), calls=%async_computation.35 | async-start | bytes 2820096
  1057.6 156.5 %reduce-scatter.47.cloned.1.call-start = ((), (), s32[]{:S(2)}) async-start(), calls=%async_computation.34 | async-start | bytes 2820096
  1061.0 257.5 %reduce-scatter.33.cloned.1.call-start = ((), (), s32[]{:S(2)}) async-start(), calls=%async_computation.19 | async-start | bytes 10653696 | tf_op jit(solution)/shard_map/reduce_scatter | solution.py:87
  1068.8 359.0 %reduce-scatter.37.cloned.1.call-start = ((), (), s32[]{:S(2)}) async-start(), calls=%async_computation.21 | async-start | bytes 11280384 | tf_op jit(solution)/shard_map/reduce_scatter | solution.py:93
  1078.8 432.4 %reduce-scatter.29.cloned.1.call-start = ((), (), s32[]{:S(2)}) async-start(), calls=%async_computation.17 | async-start | bytes 8146944 | tf_op jit(solution)/shard_map/reduce_scatter | solution.py:69
  1086.3 534.4 %reduce-scatter.35.cloned.1.call-start = ((), (), s32[]{:S(2)}) async-start(), calls=%async_computation.20 | async-start | bytes 11280384 | tf_op jit(solution)/shard_map/reduce_scatter | solution.py:93
  1095.3 630.0 %reduce-scatter.31.cloned.1.call-start = ((), (), s32[]{:S(2)}) async-start(), calls=%async_computation.18 | async-start | bytes 10653696 | tf_op jit(solution)/shard_map/reduce_scatter | solution.py:87
  1103.1 705.5 %reduce-scatter.27.cloned.1.call-start = ((), (), s32[]{:S(2)}) async-start(), calls=%async_computation.16 | async-start | bytes 8146944 | tf_op jit(solution)/shard_map/reduce_scatter | solution.py:69
  1128.4 844.1 %all-reduce.40.cloned.1.call-start = ((), (), s32[]{:S(2)}) async-start(), calls=%async_computation.36 | async-start | bytes 14622720 | tf_op jit(solution)/shard_map/psum | solution.py:106
  (118 other events, 2498.9 us)
Sparse Core Ops, SparseCore 0:
  10.3 85.3 all-gather.44
  101.4 40.6 all-gather.36
  143.8 41.6 all-gather.38
  187.0 41.5 all-gather.46
  230.7 101.8 all-gather.48
  334.6 106.0 all-gather.50
  442.4 79.9 all-gather.52
  529.4 40.7 all-gather.40
  572.4 41.6 all-gather.42
  615.6 42.0 all-gather.54
  659.3 101.5 all-gather.56
  763.0 106.0 all-gather.58
  898.2 43.5 reduce-scatter.40
  944.6 43.5 reduce-scatter.38
  1030.3 43.1 reduce-scatter.44
  1076.3 44.2 reduce-scatter.42
  1123.4 43.9 reduce-scatter.48
  1169.8 44.2 reduce-scatter.46
  1216.5 102.0 reduce-scatter.32
  1320.8 106.9 reduce-scatter.36
  1430.2 80.9 reduce-scatter.28
  1513.7 106.9 reduce-scatter.34
  1623.2 101.9 reduce-scatter.30
  1727.7 80.8 reduce-scatter.26
  1811.7 160.7 all-reduce.39
where the time goes:
time: 2000 us; the launch traced here: 1990 us
  waiting for transfers between devices  1510 us (76%)
  matrix products  196 us (10%)
  blocking collectives  136 us (7%)
  local copies, waits for them, and re-layouts  85.7 us (4%)
  other arithmetic  37.8 us (2%)
    reduce_scatter x2, waiting for transfers between devices, owner_sums(): lax.psum_scatter(terms[10].astype(jnp.bfloat16), 'shard', scatter_dimensi...  219 us
    reduce_scatter x2, waiting for transfers between devices, owner_sums(): lax.psum_scatter(terms[8].astype(jnp.bfloat16), 'shard', scatter_dimensio...  209 us
    all_gather x2, waiting for transfers between devices, fetch_forward(): lax.all_gather(pieces[10], 'shard', axis=0, tiled=True)  202 us
    all_gather x2, waiting for transfers between devices, fetch_forward(): lax.all_gather(pieces[8], 'shard', axis=0, tiled=True)  201 us
    reduce_scatter x2, waiting for transfers between devices, owner_sums(): lax.psum_scatter(terms[2].astype(jnp.bfloat16), 'shard', scatter_dimensio...  167 us
    unnamed x31, waiting for transfers between devices  156 us
    all_gather x2, waiting for transfers between devices, fetch_forward(): lax.all_gather(pieces[2], 'shard', axis=0, tiled=True)  115 us
    all_gather x2, waiting for transfers between devices, forward_layer(): lax.all_gather(key_rows, 'shard', axis=0, tiled=True)  77.1 us
  transfers between devices with their start and end apart: 25, of which 24 were waited for; matrix products, arithmetic and copies ran while one was open for 11% of the time, Pallas kernels for 0%

commit v1 on v0

v1 whole, which is shorter than its diff:
```python
import functools
import math

import jax
import jax.numpy as jnp
import numpy as np
from jax import lax
from jax.experimental import pallas as pl
from jax.experimental.pallas import tpu as pltpu
from jax.sharding import Mesh
from jax.sharding import PartitionSpec as P

HEADS = 17
HEAD_DIM = 64
LAYERS = 2
D = 1088
FF = 4352
ROWS = 144
PACK = 1152
SCALE = 1.0 / math.sqrt(HEAD_DIM)
EPS = 1e-05
ALL = ("yh", "z", "c", "yl", "x")
REP = ("yh", "z", "c")
SHARD = ("yl", "x")
BF = jnp.bfloat16
F32 = jnp.float32


def build_perm(move):
    index = np.arange(128).reshape(2, 4, 2, 2, 4)
    pairs = []
    for yh in range(2):
        for z in range(4):
            for c in range(2):
                for yl in range(2):
                    for x in range(4):
                        target = move(x, 2 * yh + yl, z, c)
                        if target is None:
                            continue
                        tx, ty, tz, tc = (value % size for value, size in zip(target, (4, 4, 4, 2)))
                        pairs.append(
                            (int(index[yh, z, c, yl, x]), int(index[ty // 2, tz, tc, ty % 2, tx]))
                        )
    return pairs


NEAR_X = build_perm(lambda x, y, z, c: (x + 1 if c == 0 else x - 1, y, z, c))
FAR_X = build_perm(lambda x, y, z, c: (x + 2, y, z, c) if c == 1 else None)
NEAR_Y = build_perm(lambda x, y, z, c: (x, y + 1 if c == 0 else y - 1, z, c))
OTHER_CORE = build_perm(lambda x, y, z, c: (x, y, z, 1 - c))


def move(array, pairs):
    return lax.ppermute(array, ALL, pairs)


def exchange(array, axes):
    return lax.all_to_all(array, axes, 0, 0, tiled=True)


def norm_rows(inputs, gain, shift):
    average = jnp.mean(inputs, axis=-1, keepdims=True)
    centered = inputs - average
    variance = jnp.mean(centered * centered, axis=-1, keepdims=True)
    return centered * lax.rsqrt(variance + EPS) * gain + shift


def gelu_tanh(inputs):
    return jax.nn.gelu(inputs, approximate=True)


def gather_blocks(own, core):
    near = move(own, NEAR_X)
    far = move(own, FAR_X)
    first = jnp.where(core == 0, own, far)
    first_y = move(first, NEAR_Y)
    near_y = move(near, NEAR_Y)
    blocks = [
        (0, 0, 2, first),
        (0, 3, 1, near),
        (1, 0, 2, first_y),
        (1, 3, 1, near_y),
        (0, 2, 0, move(first, OTHER_CORE)),
        (0, 1, 3, move(near, OTHER_CORE)),
        (1, 2, 0, move(first_y, OTHER_CORE)),
        (1, 1, 3, move(near_y, OTHER_CORE)),
    ]
    return blocks, (near, far)


def after(array, earlier):
    return lax.optimization_barrier((array, earlier))[0]


def gather_halves(zero, one, core):
    return lax.all_gather(core_half(core, zero, one), SHARD, axis=0, tiled=True)


def join_halves(half):
    both = exchange(jnp.broadcast_to(half[None], (2,) + half.shape), "c")
    return both[0], both[1]


def assemble(blocks, pick, core, y_low, x_pos, shape):
    whole = jnp.zeros((8,) + shape, BF)
    for other, offset_zero, offset_one, block in blocks:
        x_from = lax.rem(x_pos + jnp.where(core == 0, offset_zero, offset_one), 4)
        y_from = y_low if other == 0 else 1 - y_low
        whole = lax.dynamic_update_slice(
            whole, pick(block)[None], (4 * y_from + x_from,) + (0,) * len(shape)
        )
    return whole


BLOCK = 128
DOT_NT = (((1,), (1,)), ((), ()))
DOT_TN = (((0,), (0,)), ((), ()))


def dot_f32(left, right, dims=(((1,), (0,)), ((), ()))):
    return lax.dot_general(left, right, dims, preferred_element_type=F32)


def softmax_rows(queries, keys, allowed):
    scores = jnp.where(allowed, dot_f32(queries, keys, DOT_NT) * SCALE, -1e30)
    highest = jnp.max(scores, axis=-1, keepdims=True)
    exponent = jnp.exp(scores - highest)
    return exponent / jnp.sum(exponent, axis=-1, keepdims=True)


def block_mask(seg_col, seg_row, first_row, rows, keys):
    row = lax.broadcasted_iota(jnp.int32, (rows, keys), 0) + first_row
    col = lax.broadcasted_iota(jnp.int32, (rows, keys), 1)
    return (seg_col == seg_row) & (col <= row)


def attend_kernel(place, qkv, q_last, seg_col, seg_row, seg_own, out, out_last):
    for step in range(PACK // BLOCK):
        start, keys = step * BLOCK, (step + 1) * BLOCK
        allowed = block_mask(
            seg_col[start:keys, :], seg_row[:, 0:keys], start, BLOCK, keys
        )
        for head in range(2):
            lane = head * 64
            weights = softmax_rows(
                qkv[start:keys, lane : lane + 64], qkv[0:keys, 128 + lane : 192 + lane], allowed
            ).astype(BF)
            out[start:keys, lane : lane + 64] = dot_f32(
                weights, qkv[0:keys, 256 + lane : 320 + lane]
            ).astype(BF)
    allowed = block_mask(seg_own[...], seg_row[...], place[0], ROWS, PACK)
    weights = softmax_rows(q_last[:, 0:64], qkv[:, 384:448], allowed).astype(BF)
    out_last[...] = dot_f32(weights, qkv[:, 448:512]).astype(BF)


def attend_back_kernel(
    place, qkv, q_last, seg_col, seg_row, seg_own, dout, dout_last, dqkv, dq_last, dk, dv
):
    def pull(queries, keys, values, grad, allowed):
        probability = softmax_rows(queries, keys, allowed)
        grad_prob = dot_f32(grad, values, DOT_NT)
        inner = jnp.sum(grad_prob * probability, axis=-1, keepdims=True)
        grad_scores = (probability * (grad_prob - inner)).astype(BF)
        weights = probability.astype(BF)
        return (
            dot_f32(grad_scores, keys) * SCALE,
            dot_f32(grad_scores, queries, DOT_TN) * SCALE,
            dot_f32(weights, grad, DOT_TN),
        )

    dk[...] = jnp.zeros_like(dk)
    dv[...] = jnp.zeros_like(dv)
    for step in range(PACK // BLOCK):
        start, keys = step * BLOCK, (step + 1) * BLOCK
        allowed = block_mask(
            seg_col[start:keys, :], seg_row[:, 0:keys], start, BLOCK, keys
        )
        for head in range(2):
            lane = head * 64
            part_q, part_k, part_v = pull(
                qkv[start:keys, lane : lane + 64],
                qkv[0:keys, 128 + lane : 192 + lane],
                qkv[0:keys, 256 + lane : 320 + lane],
                dout[start:keys, lane : lane + 64],
                allowed,
            )
            dqkv[start:keys, lane : lane + 64] = part_q.astype(BF)
            dk[0:keys, lane : lane + 64] += part_k
            dv[0:keys, lane : lane + 64] += part_v
    dqkv[:, 128:256] = dk[...].astype(BF)
    dqkv[:, 256:384] = dv[...].astype(BF)
    allowed = block_mask(seg_own[...], seg_row[...], place[0], ROWS, PACK)
    part_q, part_k, part_v = pull(
        q_last[:, 0:64], qkv[:, 384:448], qkv[:, 448:512], dout_last[:, 0:64], allowed
    )
    dq_last[...] = part_q.astype(BF)
    dqkv[:, 384:448] = part_k.astype(BF)
    dqkv[:, 448:512] = part_v.astype(BF)


VMEM = pl.BlockSpec(memory_space=pltpu.VMEM)
SMEM = pl.BlockSpec(memory_space=pltpu.SMEM)


def attend(place, qkv, q_last, segs):
    return pl.pallas_call(
        attend_kernel,
        out_shape=(
            jax.ShapeDtypeStruct((PACK, 128), BF),
            jax.ShapeDtypeStruct((ROWS, 64), BF),
        ),
        in_specs=[SMEM] + [VMEM] * 5,
        out_specs=(VMEM, VMEM),
        compiler_params=pltpu.CompilerParams(vmem_limit_bytes=32 * 1024 * 1024),
        cost_estimate=pl.CostEstimate(flops=900_000_000, bytes_accessed=2_500_000, transcendentals=1_700_000),
        name="attend",
    )(place, qkv, q_last, *segs)


def attend_back(place, qkv, q_last, segs, dout, dout_last):
    return pl.pallas_call(
        attend_back_kernel,
        out_shape=(
            jax.ShapeDtypeStruct((PACK, 512), BF),
            jax.ShapeDtypeStruct((ROWS, 64), BF),
        ),
        in_specs=[SMEM] + [VMEM] * 7,
        out_specs=(VMEM, VMEM),
        scratch_shapes=[pltpu.VMEM((PACK, 128), F32)] * 2,
        compiler_params=pltpu.CompilerParams(vmem_limit_bytes=32 * 1024 * 1024),
        cost_estimate=pl.CostEstimate(flops=2_200_000_000, bytes_accessed=4_000_000, transcendentals=1_700_000),
        name="attend_back",
    )(place, qkv, q_last, *segs, dout, dout_last)


def by_head_pair(array):
    return array.reshape(ROWS, 8, 128).transpose(1, 0, 2)


def from_head_pair(array):
    return array.transpose(1, 0, 2).reshape(ROWS, 1024)


def times(left, weight):
    products = [jnp.dot(left, part, preferred_element_type=F32) for part in weight]
    return products[0] if len(products) == 1 else jnp.concatenate(products, axis=1)


def times_back(right, weight):
    total, start = None, 0
    for part in weight:
        product = dot_f32(right[:, start : start + part.shape[1]], part, DOT_NT)
        total = product if total is None else total + product
        start += part.shape[1]
    return total


def forward_attention(stream, small, big, place, segs):
    gain_a, shift_a, mix_bias, out_bias = small[:4]
    mix_weight, out_weight = big[:2]
    normed = norm_rows(stream, gain_a, shift_a).astype(BF)
    mixed = times(normed, mix_weight)
    queries = (mixed[:, :D] + mix_bias[:D]).astype(BF)
    key_rows = mixed[:, D : 2 * D].astype(BF)
    values = (mixed[:, 2 * D :] + mix_bias[D:]).astype(BF)
    last = jnp.concatenate([key_rows[:, 1024:], values[:, 1024:]], axis=1)
    send = jnp.concatenate(
        [
            by_head_pair(queries[:, :1024]),
            by_head_pair(key_rows[:, :1024]),
            by_head_pair(values[:, :1024]),
            jnp.broadcast_to(last[None], (8, ROWS, 128)),
        ],
        axis=2,
    )
    qkv = exchange(send, SHARD).reshape(PACK, 512)
    q_last = queries[:, 1024:]
    out, out_last = attend(place, qkv, q_last, segs)
    attended = jnp.concatenate(
        [from_head_pair(exchange(out.reshape(8, ROWS, 128), SHARD)), out_last], axis=1
    )
    stream_mid = stream + times(attended, out_weight) + out_bias
    return (stream, normed, qkv, q_last, attended), stream_mid


def forward_feed(stream_mid, small, big):
    gain_b, shift_b, up_bias, down_bias = small[4:]
    up_weight, down_weight = big[2:]
    normed_b = norm_rows(stream_mid, gain_b, shift_b).astype(BF)
    up_value = times(normed_b, up_weight) + up_bias
    active = gelu_tanh(up_value).astype(BF)
    result = stream_mid + times(active, down_weight) + down_bias
    return (stream_mid, normed_b, up_value, active), result


def both_cores(array):
    if array.shape[1] > D:
        return exchange(jnp.concatenate([array, array], axis=0), "c")
    return lax.all_gather(array, "c", axis=0, tiled=True)


def swap_halves(zero, one):
    return exchange(jnp.concatenate([zero, one], axis=0), "c")


def grad_pair(pieces):
    grads = [dot_f32(left, right, DOT_TN).astype(BF) for left, right in pieces]
    return grads[0] if len(grads) == 1 else jnp.concatenate(grads, axis=1)


def core_half(core, zero, one):
    return jnp.where(core == 0, zero, one)


def as_lanes(part):
    return part.reshape(136, FF // 2)


class SlowSum:
    def __init__(self):
        self.parts = []

    def add(self, pieces):
        self.parts.append(
            lax.psum_scatter(grad_pair(pieces), SHARD, scatter_dimension=0, tiled=True)
        )

    def finish(self, array):
        array, parts = lax.optimization_barrier((array, self.parts))
        joined = jnp.concatenate([as_lanes(part) for part in parts], axis=1)
        joined = lax.psum(joined, ("yh", "z"))
        joined = exchange(jnp.broadcast_to(joined[None], (2, 136, 3 * FF // 2)), "c")
        self.done = [joined[:, :, k * (FF // 2) : (k + 1) * (FF // 2)] for k in range(3)]
        return array


class FastSum:
    def __init__(self, core, y_low, waiting):
        self.y_low = y_low
        self.waiting = waiting
        self.sent = []
        self.parts = []

    def add(self, pieces):
        split = []
        for left, right in pieces:
            half = left.shape[1] // 2
            first, second = left[:, :half], left[:, half:]
            split.append(
                (
                    jnp.where(self.y_low == 0, second, first),
                    jnp.where(self.y_low == 0, first, second),
                    right,
                )
            )
        arrived = move(grad_pair([(other, right) for other, own, right in split]), NEAR_Y)
        self.sent.append(([(own, right) for other, own, right in split], arrived))

    def advance(self, array):
        array, arrived = lax.optimization_barrier((array, [item[1] for item in self.sent]))
        for (own, _), came in zip(self.sent, arrived):
            summed = [dot_f32(left, right, DOT_TN) for left, right in own]
            summed = summed[0] if len(summed) == 1 else jnp.concatenate(summed, axis=1)
            summed = (summed + came.astype(F32)).astype(BF)
            spread = exchange(summed, "x")
            self.parts.append(spread)
        self.sent = []
        return array

    def total(self, parts):
        summed = []
        for part in parts:
            rows = part.shape[0] // 4
            summed.append(
                as_lanes(jnp.sum(part.reshape(4, rows, -1).astype(F32), axis=0).astype(BF))
            )
        lanes = len(summed) * (FF // 2)
        wide = -(-lanes // 1024) * 1024
        summed.append(jnp.zeros((136, wide - lanes), BF))
        joined = jnp.concatenate(summed, axis=1)
        piece = wide // 8
        joined = joined.reshape(136, 8, piece).transpose(1, 0, 2)
        arrived = exchange(joined, ("yh", "z"))
        total = jnp.sum(arrived.astype(F32), axis=0).astype(BF)
        spread = exchange(jnp.broadcast_to(total[None], (16, 136, piece)), REP)
        spread = spread.reshape(8, 2, 136, piece).transpose(1, 2, 0, 3).reshape(2, 136, wide)
        return [spread[:, :, k * (FF // 2) : (k + 1) * (FF // 2)] for k in range(len(parts))]


def backward_layer(gradient, small, big, retained, place, segs, core, sums):
    gain_a, shift_a, mix_bias, out_bias, gain_b, shift_b, up_bias, down_bias = small
    mix_weight, out_weight, up_weight, down_weight = big
    stream, normed, qkv, q_last, attended, stream_mid, normed_b, up_value, active = retained
    fast = isinstance(sums, FastSum)
    grad_branch = gradient.astype(BF)
    grad_active = times_back(grad_branch, down_weight)
    gelu_pull = jax.vjp(gelu_tanh, up_value)[1]
    grad_up = gelu_pull(grad_active)[0].astype(BF)

    branch_both = both_cores(grad_branch)
    sums.add(
        [(both_cores(active), core_half(core, branch_both[:, : D // 2], branch_both[:, D // 2 :]))]
    )
    grad_normed_b = times_back(grad_up, up_weight)
    up_both = swap_halves(grad_up[:, : FF // 2], grad_up[:, FF // 2 :])
    sums.add([(both_cores(normed_b), up_both)])

    norm_pull_b = jax.vjp(norm_rows, stream_mid, gain_b, shift_b)[1]
    grad_mid_norm, grad_gain_b, grad_shift_b = norm_pull_b(grad_normed_b)
    grad_mid = gradient + grad_mid_norm
    grad_attn = grad_mid.astype(BF)
    grad_attended = times_back(grad_attn, out_weight).astype(BF)
    dout = exchange(by_head_pair(grad_attended[:, :1024]), SHARD).reshape(PACK, 128)
    if fast:
        dout = sums.advance(dout)
    dqkv, dq_last = attend_back(place, qkv, q_last, segs, dout, grad_attended[:, 1024:])
    arrived = exchange(dqkv.reshape(8, ROWS, 512), SHARD)
    if fast:
        arrived, sums.parts = lax.optimization_barrier((arrived, sums.parts))
        down_sum, up_sum = sums.total(sums.parts)
        sums.parts = []
    last = jnp.sum(arrived[:, :, 384:].astype(F32), axis=0).astype(BF)
    grad_queries = jnp.concatenate([from_head_pair(arrived[:, :, 0:128]), dq_last], axis=1)
    grad_keys = jnp.concatenate([from_head_pair(arrived[:, :, 128:256]), last[:, :64]], axis=1)
    grad_values = jnp.concatenate([from_head_pair(arrived[:, :, 256:384]), last[:, 64:]], axis=1)
    grad_mixed = jnp.concatenate([grad_queries, grad_keys, grad_values], axis=1)

    if fast:
        grad_mixed = sums.waiting.finish(grad_mixed)
    normed_both = both_cores(normed)
    attended_both = both_cores(attended)
    right = swap_halves(
        grad_mixed[:, : 2 * D], jnp.concatenate([grad_values, grad_attn], axis=1)
    )
    sums.add(
        [
            (normed_both, right[:, :D]),
            (core_half(core, normed_both, attended_both), right[:, D:]),
        ]
    )
    grad_normed = times_back(grad_mixed, mix_weight)
    norm_pull_a = jax.vjp(norm_rows, stream, gain_a, shift_a)[1]
    grad_in_norm, grad_gain_a, grad_shift_a = norm_pull_a(grad_normed)
    grad_in = grad_mid + grad_in_norm
    if fast:
        sums.advance(dout)
        owned_big = (sums.total(sums.parts)[0], up_sum, down_sum)
    else:
        owned_big = None
    small_grads = (
        grad_gain_a,
        grad_shift_a,
        jnp.concatenate(
            [jnp.sum(grad_queries.astype(F32), axis=0), jnp.sum(grad_values.astype(F32), axis=0)]
        ),
        jnp.sum(grad_attn.astype(F32), axis=0),
        grad_gain_b,
        grad_shift_b,
        jnp.sum(grad_up.astype(F32), axis=0),
        jnp.sum(grad_branch.astype(F32), axis=0),
    )
    small_grads = jnp.concatenate([vector.reshape(8, -1) for vector in small_grads], axis=1)
    return grad_in, owned_big, small_grads


SMALL_WIDTHS = (136, 136, 272, 136, 136, 136, 544, 136)
SMALL = sum(SMALL_WIDTHS)
SMALL_EDGES = [sum(SMALL_WIDTHS[:index]) for index in range(9)]


def body(
    tokens,
    cotangent,
    segments,
    gain_one,
    shift_one,
    w_qkv,
    bias_qv,
    w_out,
    bias_out,
    gain_two,
    shift_two,
    w_up,
    bias_up,
    w_down,
    bias_down,
):
    core = lax.axis_index("c")
    y_low = lax.axis_index("yl")
    x_pos = lax.axis_index("x")
    member = 4 * y_low + x_pos
    place = (member * ROWS).astype(jnp.int32).reshape(1)
    seg_own = lax.dynamic_slice_in_dim(segments, member * ROWS, ROWS)
    segs = (segments[:, None], segments[None, :], seg_own[:, None])

    vectors = (gain_one, shift_one, bias_qv, bias_out, gain_two, shift_two, bias_up, bias_down)
    own_small = jnp.concatenate(vectors, axis=1)
    all_small = exchange(jnp.broadcast_to(own_small[None], (8, LAYERS, SMALL)), SHARD)
    smalls = []
    for depth in range(LAYERS):
        smalls.append(
            tuple(
                all_small[:, depth, SMALL_EDGES[k] : SMALL_EDGES[k + 1]].reshape(-1).astype(F32)
                for k in range(8)
            )
        )

    put = functools.partial(assemble, core=core, y_low=y_low, x_pos=x_pos)
    blocks, came = gather_blocks(jnp.concatenate([w_qkv[0], w_out[0]], axis=1), core)
    mix = put(blocks, lambda b: b[:, : 3 * D], shape=(136, 3 * D)).reshape(D, 3 * D)
    out = put(blocks, lambda b: b[:, 3 * D :], shape=(136, D)).reshape(D, D)
    later = after((w_qkv[1], w_out[1], w_up[1], w_down[1]), came)
    blocks, came = gather_blocks(after(w_up[0], came), core)
    up = put(blocks, lambda b: b, shape=(136, FF)).reshape(D, FF)
    blocks, came = gather_blocks(after(w_down[0], came), core)
    down = put(blocks, lambda b: b, shape=(544, D)).reshape(FF, D)
    bigs = [((mix,), (out,), (up,), (down,))]
    halves = [
        gather_halves(
            later[0][:, : 2 * D], jnp.concatenate([later[0][:, 2 * D :], later[1]], axis=1), core
        ),
        gather_halves(later[2][:, : FF // 2], later[2][:, FF // 2 :], core),
        gather_halves(later[3][:, : D // 2], later[3][:, D // 2 :], core),
    ]

    stream = tokens.astype(F32)
    stored = []
    retained, mid = forward_attention(stream, smalls[0], bigs[0], place, segs)
    mid, halves[0] = lax.optimization_barrier((mid, halves[0]))
    zero, one = join_halves(halves[0])
    rest, stream = forward_feed(mid, smalls[0], bigs[0])
    stored.append(retained + rest)
    stream, halves[1] = lax.optimization_barrier((stream, halves[1]))
    second = [(zero, one[:, :D]), (one[:, D:],), join_halves(halves[1])]
    retained, mid = forward_attention(stream, smalls[1], second, place, segs)
    mid, halves[2] = lax.optimization_barrier((mid, halves[2]))
    second.append(join_halves(halves[2]))
    rest, stream = forward_feed(mid, smalls[1], second)
    stored.append(retained + rest)
    bigs.append(second)
    output = stream.astype(BF)

    gradient = cotangent.astype(F32)
    owned, small_grads = [None] * LAYERS, [None] * LAYERS
    slow = SlowSum()
    fast = FastSum(core, y_low, slow)
    for depth, sums in ((1, slow), (0, fast)):
        gradient, owned[depth], small_grads[depth] = backward_layer(
            gradient, smalls[depth], bigs[depth], stored[depth], place, segs, core, sums
        )
    down_sum, up_sum, mix_sum = slow.done
    owned[1] = (mix_sum, up_sum, down_sum)

    small_sum = jnp.sum(
        exchange(jnp.stack(small_grads, axis=1), SHARD).reshape(8, LAYERS, SMALL), axis=0
    )
    small_sum = jnp.sum(
        exchange(jnp.broadcast_to(small_sum[None], (16, LAYERS, SMALL)), REP), axis=0
    )
    small_out = [small_sum[:, SMALL_EDGES[k] : SMALL_EDGES[k + 1]] for k in range(8)]

    def stack(build):
        return jnp.stack([build(*owned[depth]) for depth in range(LAYERS)]).astype(F32)

    grad_qkv = stack(lambda mix, up, down: jnp.concatenate([mix[0], mix[1, :, :D]], axis=1))
    grad_out = stack(lambda mix, up, down: mix[1, :, D:])
    grad_up = stack(lambda mix, up, down: jnp.concatenate([up[0], up[1]], axis=1))
    grad_down = stack(lambda mix, up, down: jnp.concatenate([half.reshape(544, D // 2) for half in down], axis=1))
    return (
        output,
        gradient.astype(BF),
        small_out[0],
        small_out[1],
        grad_qkv,
        small_out[2],
        grad_out,
        small_out[3],
        small_out[4],
        small_out[5],
        grad_up,
        small_out[6],
        grad_down,
        small_out[7],
    )


def solution(mesh):
    fine = Mesh(mesh.devices.reshape(2, 4, 2, 2, 4), ALL)
    rows = P(ALL, None)
    vector = P(None, SHARD)
    matrix = P(None, SHARD, None)
    in_specs = (
        rows,
        rows,
        P(REP),
        vector,
        vector,
        matrix,
        vector,
        matrix,
        vector,
        vector,
        vector,
        matrix,
        vector,
        matrix,
        vector,
    )
    out_specs = (rows, rows) + in_specs[3:]
    return jax.shard_map(body, mesh=fine, in_specs=in_specs, out_specs=out_specs, check_vma=False)
```

time: 2000 us -> 1150 us (0.57)
  waiting for transfers between devices: 1510 us -> 369 us
  starting transfers between devices: 1.77 us -> 202 us
  local copies, waits for them, and re-layouts: 85.7 us -> 202 us
  matrix products: 196 us -> 125 us
  blocking collectives: 136 us -> 82.8 us
  Pallas kernels: 0 us -> 51.5 us
  other arithmetic: 37.8 us -> 89 us
    all_gather x12 -> x3, waiting for transfers between devices: 718 us -> 0.02 us  [gather_halves(): return lax.all_gather(core_half(core, zero, one), SHARD, axis=0, tiled=True)]
    reduce_scatter x6 -> x1, waiting for transfers between devices: 595 us -> 0.01 us  [add(): lax.psum_scatter(grad_pair(pieces), SHARD, scatter_dimension=0, tiled=True)]
    all_to_all x0 -> x22, waiting for transfers between devices: none -> 239 us  [exchange(): return lax.all_to_all(array, axes, 0, 0, tiled=True)]
    unnamed x31 -> x7, waiting for transfers between devices: 156 us -> 0.11 us
    all_to_all x0 -> x22, starting transfers between devices: none -> 113 us  [exchange(): return lax.all_to_all(array, axes, 0, 0, tiled=True)]
    ppermute x0 -> x27, starting transfers between devices: none -> 89.6 us  [move(): return lax.ppermute(array, ALL, pairs)]
    ppermute x0 -> x27, waiting for transfers between devices: none -> 83 us  [move(): return lax.ppermute(array, ALL, pairs)]
    unnamed x2 -> x0, blocking collectives: 71 us -> none
  transfers between devices with their start and end apart: 25 -> 56, of which waited for: 24 -> 18; matrix products, arithmetic and copies ran while one was open for 11% -> 31% of each run, Pallas kernels for 0% -> 5%
where the time goes in v1:
time: 1150 us; the launch traced here: 1140 us
  waiting for transfers between devices  369 us (32%)
  starting transfers between devices  202 us (18%)
  local copies, waits for them, and re-layouts  202 us (18%)
  matrix products  125 us (11%)
  other arithmetic  89 us (8%)
  blocking collectives  82.8 us (7%)
  Pallas kernels  51.5 us (4%)
  between operations  16.9 us (1%)
    all_to_all x22, waiting for transfers between devices, exchange(): return lax.all_to_all(array, axes, 0, 0, tiled=True)  239 us
    all_to_all x22, starting transfers between devices, exchange(): return lax.all_to_all(array, axes, 0, 0, tiled=True)  113 us
    ppermute x27, starting transfers between devices, move(): return lax.ppermute(array, ALL, pairs)  89.6 us
    dot_general x23, matrix products, dot_f32(): return lax.dot_general(left, right, dims, preferred_element_type=F32)  85.2 us
    ppermute x27, waiting for transfers between devices, move(): return lax.ppermute(array, ALL, pairs)  83 us
    all_to_all x6, blocking collectives, exchange(): return lax.all_to_all(array, axes, 0, 0, tiled=True)  63.3 us
    dynamic_update_slice x30, local copies, waits for them, and re-layouts, assemble(): lax.dynamic_update_slice(whole, pick(block)[None], (4 * y_from + x_from,)...  52.6 us
    psum x1, waiting for transfers between devices, finish(): joined = lax.psum(joined, ('yh', 'z'))  46.6 us
  transfers between devices with their start and end apart: 56, of which 18 were waited for; matrix products, arithmetic and copies ran while one was open for 31% of the time, Pallas kernels for 5%

profile of v1, /device:TPU:0, one launch (start us, length us, event | category | flops | bytes accessed | tf_op | source)
XLA Modules:
  0.0 1138.7 jit_solution(11841609843430562109)
XLA Ops:
  21.4 21.9 %collective-permute-done.1 = bf16[136,4352]{1,0:T(8,128)(2,1)} collective-permute-done((bf16[136,4352]{1,0:T(8,128)(2,1)}, bf16[136,4352]{1,0:T(8,128)(2,1)}, u32[]{:S(2)}, u32[]{:S(2)}) %collective-permute-start.1) | collective-permute-done | bytes 1183776 | tf_op jit(solution)/shard_map/ppermute | solution.py:54
  94.2 34.0 %collective-permute-start.5 = (bf16[136,4352]{1,0:T(8,128)(2,1)}, bf16[136,4352]{1,0:T(8,128)(2,1)S(1)}, u32[]{:S(2)}, u32[]{:S(2)}) collective-permute-start(bf16[136,4352]{1,0:T(8,128)(2,1)} %collective-permute-done.1), channel_id=1, source_target_pairs={{0,8},{1,9},{2,10},{3,11},{4,12},{5,13},{6,14},{7,15},{8,0},{9,1},... | collective-permute-start | bytes 3551240 | tf_op jit(solution)/shard_map/ppermute | solution.py:54
  162.2 32.6 %collective-permute-start.13 = (bf16[136,4352]{1,0:T(8,128)(2,1)}, bf16[136,4352]{1,0:T(8,128)(2,1)S(1)}, u32[]{:S(2)}, u32[]{:S(2)}) collective-permute-start(bf16[136,4352]{1,0:T(8,128)(2,1)} %collective-permute-done.9), channel_id=1, source_target_pairs={{0,8},{1,9},{2,10},{3,11},{4,12},{5,13},{6,14},{7,15},{8,0},{9,1},... | collective-permute-start | bytes 3551240 | tf_op jit(solution)/shard_map/ppermute | solution.py:54
  222.4 9.0 attend.2
  238.2 61.0 %collective-permute-done.19 = bf16[544,1088]{1,0:T(8,128)(2,1)} collective-permute-done((bf16[544,1088]{1,0:T(8,128)(2,1)}, bf16[544,1088]{1,0:T(8,128)(2,1)}, u32[]{:S(2)}, u32[]{:S(2)}) %collective-permute-start.19) | collective-permute-done | bytes 1183776 | tf_op jit(solution)/shard_map/ppermute | solution.py:54
  321.1 7.3 multiply_convert_fusion.1
  335.4 6.6 broadcast_in_dim.284
  342.0 7.5 all-to-all-start.3
  350.0 7.7 all-to-all-done.3
  372.8 16.8 %all-to-all-done.4 = bf16[8,144,512]{2,1,0:T(8,128)(2,1)S(1)} async-done(((bf16[8,144,512]{2,1,0:T(8,128)(2,1)}), bf16[8,144,512]{2,1,0:T(8,128)(2,1)S(1)}, u32[]{:S(2)}, u32[]{:S(2)}) %all-to-all-start.4) | async-done | bytes 1179680 | tf_op jit(solution)/shard_map/all_to_all | solution.py:58
  389.6 9.0 attend.3
  417.1 7.4 all-to-all-start.6
  456.5 7.7 copy.187
  470.8 13.0 %all_to_all.201 = bf16[2,4352,544]{1,2,0:T(8,128)(2,1)S(1)} all-to-all(bf16[2,4352,544]{1,2,0:T(8,128)(2,1)} %broadcast_in_dim.287), channel_id=1, replica_groups=mesh['yh'=2,'z'=4,'c'=2,'yl'=2,'x'=4] {'c'}, dimensions={0} | all-to-all | bytes 18939904 | tf_op jit(solution)/shard_map/all_to_all | solution.py:58
  512.9 7.8 all-to-all-done.8
  525.6 16.7 %attend_back.2 = (bf16[1152,512]{1,0:T(8,128)(2,1)}, bf16[144,64]{1,0:T(8,128)(2,1)S(1)}) custom-call(s32[1]{0:T(128)} %bitcast.place, bf16[1152,512]{1,0:T(8,128)(2,1)S(1)} %bitcast.369, bf16[144,64]{1,0:T(8,128)(2,1)S(1)} %slice.617.q_last, s32[1152,1]{1,0:T(8,128)S(1)} %broadcast_in_dim.301.seg_col, s32[1,1152]{1,0:T(1,128)S(1)} %broadcast_in_dim.255.seg_row, ...), custom_call_target="tpu_custom_call" | custom-call | flops 2200000000 | bytes 4000000 | tf_op jit(solution)/shard_map/attend_back/pallas_call | solution.py:221
  595.4 7.9 convert_reduce_fusion.1
  641.7 31.2 %all-to-all-done.10 = bf16[8,144,128]{2,1,0:T(8,128)(2,1)S(1)} async-done(((bf16[8,144,128]{2,1,0:T(8,128)(2,1)}), bf16[8,144,128]{2,1,0:T(8,128)(2,1)S(1)}, u32[]{:S(2)}, u32[]{:S(2)}) %all-to-all-start.10) | async-done | bytes 294944 | tf_op jit(solution)/shard_map/all_to_all | solution.py:58
  672.9 16.8 %attend_back.3 = (bf16[1152,512]{1,0:T(8,128)(2,1)}, bf16[144,64]{1,0:T(8,128)(2,1)S(1)}) custom-call(s32[1]{0:T(128)} %bitcast.place, bf16[1152,512]{1,0:T(8,128)(2,1)S(1)} %bitcast.367, bf16[144,64]{1,0:T(8,128)(2,1)S(1)} %slice.589.q_last, s32[1152,1]{1,0:T(8,128)S(1)} %broadcast_in_dim.301.seg_col, s32[1,1152]{1,0:T(1,128)S(1)} %broadcast_in_dim.255.seg_row, ...), custom_call_target="tpu_custom_call" | custom-call | flops 2200000000 | bytes 4000000 | tf_op jit(solution)/shard_map/attend_back/pallas_call | solution.py:221
  704.1 6.8 all_to_all.145
  732.3 36.0 %all-to-all-done.14 = bf16[4,544,544]{1,2,0:T(8,128)(2,1)} async-done(((bf16[4,544,544]{1,2,0:T(8,128)(2,1)}), bf16[4,544,544]{1,2,0:T(8,128)(2,1)}, u32[]{:S(2)}, u32[]{:S(2)}) %all-to-all-start.14) | async-done | bytes 2367520 | tf_op jit(solution)/shard_map/all_to_all | solution.py:58
  783.5 39.8 %all-to-all-done.15 = bf16[4,136,2176]{2,1,0:T(8,128)(2,1)} async-done(((bf16[4,136,2176]{2,1,0:T(8,128)(2,1)}), bf16[4,136,2176]{2,1,0:T(8,128)(2,1)}, u32[]{:S(2)}, u32[]{:S(2)}) %all-to-all-start.15) | async-done | bytes 2367520 | tf_op jit(solution)/shard_map/all_to_all | solution.py:58
  825.3 6.8 reshape.506
  839.2 26.0 %all_to_all.203 = bf16[8,136,640]{2,1,0:T(8,128)(2,1)S(1)} all-to-all(bf16[8,136,640]{2,1,0:T(8,128)(2,1)S(1)} %copy.206), channel_id=1, replica_groups=mesh['yh'=2,'z'=4,'c'=2,'yl'=2,'x'=4] {'yh','z'}, dimensions={0} | all-to-all | bytes 2785280 | tf_op jit(solution)/shard_map/all_to_all | solution.py:58
  884.5 24.8 %all-to-all-done.27 = bf16[16,136,640]{2,1,0:T(8,128)(2,1)} async-done(((bf16[16,136,640]{2,1,0:T(8,128)(2,1)}), bf16[16,136,640]{2,1,0:T(8,128)(2,1)}, u32[]{:S(2)}, u32[]{:S(2)}) %all-to-all-start.27) | async-done | bytes 2785312 | tf_op jit(solution)/shard_map/all_to_all | solution.py:58
  949.2 14.9 %all-to-all-done.19 = f32[8,2,1632]{2,1,0:T(2,128)S(1)} async-done(((f32[8,2,1632]{2,1,0:T(2,128)}), f32[8,2,1632]{2,1,0:T(2,128)S(1)}, u32[]{:S(2)}, u32[]{:S(2)}) %all-to-all-start.19) | async-done | bytes 104480 | tf_op jit(solution)/shard_map/all_to_all | solution.py:58
  964.9 12.7 %all-to-all-start.20 = ((f32[16,2,1632]{2,1,0:T(2,128)}), f32[16,2,1632]{2,1,0:T(2,128)S(1)}, u32[]{:S(2)}, u32[]{:S(2)}) async-start(f32[16,2,1632]{2,1,0:T(2,128)} %broadcast_in_dim.296), calls=%async_computation.21 | async-start | bytes 425984 | tf_op jit(solution)/shard_map/all_to_all | solution.py:58
  987.7 46.6 %all-reduce.5.cloned.1.call-done = bf16[136,6528]{1,0:T(8,128)(2,1)} async-done(((bf16[136,6528]{1,0:T(8,128)(2,1)}), bf16[136,6528]{1,0:T(8,128)(2,1)}) %all-reduce.5.cloned.1.call-update) | async-done | bytes 1775632 | tf_op jit(solution)/shard_map/psum | solution.py:331
  1035.9 7.6 all_to_all.205
  1063.0 14.4 %all-to-all-done.22 = bf16[4,136,2176]{2,1,0:T(8,128)(2,1)S(1)} async-done(((bf16[4,136,2176]{2,1,0:T(8,128)(2,1)}), bf16[4,136,2176]{2,1,0:T(8,128)(2,1)S(1)}, u32[]{:S(2)}, u32[]{:S(2)}) %all-to-all-start.22) | async-done | bytes 2367520 | tf_op jit(solution)/shard_map/all_to_all | solution.py:58
  1086.3 11.7 %all-to-all-done.23 = bf16[8,136,384]{2,1,0:T(8,128)(2,1)S(1)} async-done(((bf16[8,136,384]{2,1,0:T(8,128)(2,1)}), bf16[8,136,384]{2,1,0:T(8,128)(2,1)S(1)}, u32[]{:S(2)}, u32[]{:S(2)}) %all-to-all-start.23) | async-done | bytes 835616 | tf_op jit(solution)/shard_map/all_to_all | solution.py:58
  1111.3 16.6 %all-to-all-done.24 = bf16[16,136,384]{2,1,0:T(8,128)(2,1)S(1)} async-done(((bf16[16,136,384]{2,1,0:T(8,128)(2,1)}), bf16[16,136,384]{2,1,0:T(8,128)(2,1)S(1)}, u32[]{:S(2)}, u32[]{:S(2)}) %all-to-all-start.24) | async-done | bytes 1671200 | tf_op jit(solution)/shard_map/all_to_all | solution.py:58
  (687 shorter events, 535.1 us)
Async XLA Ops:
  7.2 313.3 %all-gather.4.cloned.1.call-start = ((), (), s32[]{:S(2)}) async-start(), calls=%async_computation.31 | async-start | bytes 5326848 | tf_op jit(solution)/shard_map/all_gather | solution.py:96
  44.6 290.6 %all-gather.6.cloned.1.call-start = ((), (), s32[]{:S(2)}) async-start(), calls=%async_computation.32 | async-start | bytes 5326848 | tf_op jit(solution)/shard_map/all_gather | solution.py:96
  52.4 377.7 %all-gather.8.cloned.1.call-start = ((), (), s32[]{:S(2)}) async-start(), calls=%async_computation.33 | async-start | bytes 6266880 | tf_op jit(solution)/shard_map/all_gather | solution.py:96
  77.6 53.9 %collective-permute-start.2 = (bf16[136,4352]{1,0:T(8,128)(2,1)}, bf16[136,4352]{1,0:T(8,128)(2,1)}, u32[]{:S(2)}, u32[]{:S(2)}) collective-permute-start(bf16[136,4352]{1,0:T(8,128)(2,1)} %broadcast_select_fusion.2), channel_id=1, source_target_pairs={{0,4},{1,5},{2,6},{3,7},{4,64},{5,65},{6,66},{7,67},{8,76},{9,77},... | collective-permute-start | bytes 3551240 | tf_op jit(solution)/shard_map/ppermute | solution.py:54
  78.1 62.0 %collective-permute-start.4 = (bf16[136,4352]{1,0:T(8,128)(2,1)}, bf16[136,4352]{1,0:T(8,128)(2,1)}, u32[]{:S(2)}, u32[]{:S(2)}) collective-permute-start(bf16[136,4352]{1,0:T(8,128)(2,1)} %broadcast_select_fusion.2), channel_id=1, source_target_pairs={{0,8},{1,9},{2,10},{3,11},{4,12},{5,13},{6,14},{7,15},{8,0},{9,1},... | collective-permute-start | bytes 3551240 | tf_op jit(solution)/shard_map/ppermute | solution.py:54
  81.3 55.0 %collective-permute-start.9 = (bf16[136,4352]{1,0:T(8,128)(2,1)}, bf16[136,4352]{1,0:T(8,128)(2,1)}, u32[]{:S(2)}, u32[]{:S(2)}) collective-permute-start(bf16[136,4352]{1,0:T(8,128)(2,1)} %get-tuple-element.50), channel_id=1, source_target_pairs={{0,1},{1,2},{2,3},{3,0},{4,5},{5,6},{6,7},{7,4},{8,11},{9,8},{10,9... | collective-permute-start | bytes 3551240 | tf_op jit(solution)/shard_map/ppermute | solution.py:54
  90.0 47.4 %collective-permute-start.3 = (bf16[136,4352]{1,0:T(8,128)(2,1)}, bf16[136,4352]{1,0:T(8,128)(2,1)S(1)}, u32[]{:S(2)}, u32[]{:S(2)}) collective-permute-start(bf16[136,4352]{1,0:T(8,128)(2,1)} %collective-permute-done.1), channel_id=1, source_target_pairs={{0,4},{1,5},{2,6},{3,7},{4,64},{5,65},{6,66},{7,67},{8,76},{9,77},... | collective-permute-start | bytes 3551240 | tf_op jit(solution)/shard_map/ppermute | solution.py:54
  94.2 50.0 %collective-permute-start.5 = (bf16[136,4352]{1,0:T(8,128)(2,1)}, bf16[136,4352]{1,0:T(8,128)(2,1)S(1)}, u32[]{:S(2)}, u32[]{:S(2)}) collective-permute-start(bf16[136,4352]{1,0:T(8,128)(2,1)} %collective-permute-done.1), channel_id=1, source_target_pairs={{0,8},{1,9},{2,10},{3,11},{4,12},{5,13},{6,14},{7,15},{8,0},{9,1},... | collective-permute-start | bytes 3551240 | tf_op jit(solution)/shard_map/ppermute | solution.py:54
  131.5 70.9 %collective-permute-start.10 = (bf16[136,4352]{1,0:T(8,128)(2,1)}, bf16[136,4352]{1,0:T(8,128)(2,1)}, u32[]{:S(2)}, u32[]{:S(2)}) collective-permute-start(bf16[136,4352]{1,0:T(8,128)(2,1)} %get-tuple-element.125), channel_id=1, source_target_pairs={{0,4},{1,5},{2,6},{3,7},{4,64},{5,65},{6,66},{7,67},{8,76},{9,77},... | collective-permute-start | bytes 3551240 | tf_op jit(solution)/shard_map/ppermute | solution.py:54
  136.3 71.9 %collective-permute-start.12 = (bf16[136,4352]{1,0:T(8,128)(2,1)}, bf16[136,4352]{1,0:T(8,128)(2,1)}, u32[]{:S(2)}, u32[]{:S(2)}) collective-permute-start(bf16[136,4352]{1,0:T(8,128)(2,1)} %get-tuple-element.125), channel_id=1, source_target_pairs={{0,8},{1,9},{2,10},{3,11},{4,12},{5,13},{6,14},{7,15},{8,0},{9,1},... | collective-permute-start | bytes 3551240 | tf_op jit(solution)/shard_map/ppermute | solution.py:54
  147.3 63.8 %collective-permute-start.17 = (bf16[544,1088]{1,0:T(8,128)(2,1)}, bf16[544,1088]{1,0:T(8,128)(2,1)}, u32[]{:S(2)}, u32[]{:S(2)}) collective-permute-start(bf16[544,1088]{1,0:T(8,128)(2,1)} %get-tuple-element.51), channel_id=1, source_target_pairs={{0,1},{1,2},{2,3},{3,0},{4,5},{5,6},{6,7},{7,4},{8,11},{9,8},{10,9... | collective-permute-start | bytes 3551240 | tf_op jit(solution)/shard_map/ppermute | solution.py:54
  148.6 57.1 %collective-permute-start.11 = (bf16[136,4352]{1,0:T(8,128)(2,1)}, bf16[136,4352]{1,0:T(8,128)(2,1)}, u32[]{:S(2)}, u32[]{:S(2)}) collective-permute-start(bf16[136,4352]{1,0:T(8,128)(2,1)} %collective-permute-done.9), channel_id=1, source_target_pairs={{0,4},{1,5},{2,6},{3,7},{4,64},{5,65},{6,66},{7,67},{8,76},{9,77},... | collective-permute-start | bytes 3551240 | tf_op jit(solution)/shard_map/ppermute | solution.py:54
  157.2 65.2 %all-to-all-start.1 = ((bf16[8,144,512]{2,1,0:T(8,128)(2,1)}), bf16[8,144,512]{2,1,0:T(8,128)(2,1)S(1)}, u32[]{:S(2)}, u32[]{:S(2)}) async-start(bf16[8,144,512]{2,1,0:T(8,128)(2,1)} %pad_maximum_fusion.10), calls=%async_computation.1 | async-start | bytes 2359296 | tf_op jit(solution)/shard_map/all_to_all | solution.py:58
  162.2 48.9 %collective-permute-start.13 = (bf16[136,4352]{1,0:T(8,128)(2,1)}, bf16[136,4352]{1,0:T(8,128)(2,1)S(1)}, u32[]{:S(2)}, u32[]{:S(2)}) collective-permute-start(bf16[136,4352]{1,0:T(8,128)(2,1)} %collective-permute-done.9), channel_id=1, source_target_pairs={{0,8},{1,9},{2,10},{3,11},{4,12},{5,13},{6,14},{7,15},{8,0},{9,1},... | collective-permute-start | bytes 3551240 | tf_op jit(solution)/shard_map/ppermute | solution.py:54
  205.8 97.4 %collective-permute-start.20 = (bf16[544,1088]{1,0:T(8,128)(2,1)}, bf16[544,1088]{1,0:T(8,128)(2,1)}, u32[]{:S(2)}, u32[]{:S(2)}) collective-permute-start(bf16[544,1088]{1,0:T(8,128)(2,1)} %get-tuple-element.123), channel_id=1, source_target_pairs={{0,8},{1,9},{2,10},{3,11},{4,12},{5,13},{6,14},{7,15},{8,0},{9,1},... | collective-permute-start | bytes 3551240 | tf_op jit(solution)/shard_map/ppermute | solution.py:54
  208.2 97.5 %collective-permute-start.14 = (bf16[136,4352]{1,0:T(8,128)(2,1)}, bf16[136,4352]{1,0:T(8,128)(2,1)}, u32[]{:S(2)}, u32[]{:S(2)}) collective-permute-start(bf16[136,4352]{1,0:T(8,128)(2,1)} %collective-permute-done.10), channel_id=1, source_target_pairs={{0,8},{1,9},{2,10},{3,11},{4,12},{5,13},{6,14},{7,15},{8,0},{9,1},... | collective-permute-start | bytes 3551240 | tf_op jit(solution)/shard_map/ppermute | solution.py:54
  211.0 97.1 %collective-permute-start.15 = (bf16[136,4352]{1,0:T(8,128)(2,1)}, bf16[136,4352]{1,0:T(8,128)(2,1)}, u32[]{:S(2)}, u32[]{:S(2)}) collective-permute-start(bf16[136,4352]{1,0:T(8,128)(2,1)} %collective-permute-done.11), channel_id=1, source_target_pairs={{0,8},{1,9},{2,10},{3,11},{4,12},{5,13},{6,14},{7,15},{8,0},{9,1},... | collective-permute-start | bytes 3551240 | tf_op jit(solution)/shard_map/ppermute | solution.py:54
  211.1 88.1 %collective-permute-start.19 = (bf16[544,1088]{1,0:T(8,128)(2,1)}, bf16[544,1088]{1,0:T(8,128)(2,1)}, u32[]{:S(2)}, u32[]{:S(2)}) collective-permute-start(bf16[544,1088]{1,0:T(8,128)(2,1)} %collective-permute-done.17), channel_id=1, source_target_pairs={{0,4},{1,5},{2,6},{3,7},{4,64},{5,65},{6,66},{7,67},{8,76},{9,77},... | collective-permute-start | bytes 3551240 | tf_op jit(solution)/shard_map/ppermute | solution.py:54
  231.4 80.3 %all-to-all-start.2 = ((bf16[8,144,128]{2,1,0:T(8,128)(2,1)}), bf16[8,144,128]{2,1,0:T(8,128)(2,1)}, u32[]{:S(2)}, u32[]{:S(2)}) async-start(bf16[8,144,128]{2,1,0:T(8,128)(2,1)} %bitcast.17), calls=%async_computation.2 | async-start | bytes 589824 | tf_op jit(solution)/shard_map/all_to_all | solution.py:58
  235.4 75.1 %collective-permute-start.21 = (bf16[544,1088]{1,0:T(8,128)(2,1)}, bf16[544,1088]{1,0:T(8,128)(2,1)S(1)}, u32[]{:S(2)}, u32[]{:S(2)}) collective-permute-start(bf16[544,1088]{1,0:T(8,128)(2,1)} %collective-permute-done.17), channel_id=1, source_target_pairs={{0,8},{1,9},{2,10},{3,11},{4,12},{5,13},{6,14},{7,15},{8,0},{9,1},... | collective-permute-start | bytes 3551240 | tf_op jit(solution)/shard_map/ppermute | solution.py:54
  424.5 493.6 %reduce-scatter.10.cloned.1.call-start = ((), (), s32[]{:S(2)}) async-start(), calls=%async_computation.34 | async-start | bytes 6266880 | tf_op jit(solution)/shard_map/reduce_scatter | solution.py:325
  547.0 371.1 %reduce-scatter.12.cloned.1.call-start = ((), (), s32[]{:S(2)}) async-start(), calls=%async_computation.36 | async-start | bytes 5326848
  593.2 79.7 %collective-permute-start.24 = (bf16[2176,544]{0,1:T(8,128)(2,1)}, bf16[2176,544]{0,1:T(8,128)(2,1)}, u32[]{:S(2)}, u32[]{:S(2)}) collective-permute-start(bf16[2176,544]{0,1:T(8,128)(2,1)} %convolution_convert_fusion.5), channel_id=1, source_target_pairs={{0,4},{1,5},{2,6},{3,7},{4,64},{5,65},{6,66},{7,67},{8,76},{9,77},... | collective-permute-start | bytes 7102472 | tf_op jit(solution)/shard_map/ppermute | solution.py:54
  612.2 60.7 %collective-permute-start.25 = (bf16[544,2176]{1,0:T(8,128)(2,1)}, bf16[544,2176]{1,0:T(8,128)(2,1)}, u32[]{:S(2)}, u32[]{:S(2)}) collective-permute-start(bf16[544,2176]{1,0:T(8,128)(2,1)} %convolution_convert_fusion.4), channel_id=1, source_target_pairs={{0,4},{1,5},{2,6},{3,7},{4,64},{5,65},{6,66},{7,67},{8,76},{9,77},... | collective-permute-start | bytes 7102472 | tf_op jit(solution)/shard_map/ppermute | solution.py:54
  631.4 41.6 %all-to-all-start.10 = ((bf16[8,144,128]{2,1,0:T(8,128)(2,1)}), bf16[8,144,128]{2,1,0:T(8,128)(2,1)S(1)}, u32[]{:S(2)}, u32[]{:S(2)}) async-start(bf16[8,144,128]{2,1,0:T(8,128)(2,1)} %bitcast_bitcast_fusion), calls=%async_computation.10 | async-start | bytes 589824 | tf_op jit(solution)/shard_map/all_to_all | solution.py:58
  714.6 53.7 %all-to-all-start.14 = ((bf16[4,544,544]{1,2,0:T(8,128)(2,1)}), bf16[4,544,544]{1,2,0:T(8,128)(2,1)}, u32[]{:S(2)}, u32[]{:S(2)}) async-start(bf16[4,544,544]{1,2,0:T(8,128)(2,1)} %copy.197), calls=%async_computation.14 | async-start | bytes 5570560 | tf_op jit(solution)/shard_map/all_to_all | solution.py:58
  719.4 198.7 %reduce-scatter.14.cloned.1.call-start = ((), (), s32[]{:S(2)}) async-start(), calls=%async_computation.37 | async-start | bytes 5326848
  768.3 55.0 %all-to-all-start.15 = ((bf16[4,136,2176]{2,1,0:T(8,128)(2,1)}), bf16[4,136,2176]{2,1,0:T(8,128)(2,1)}, u32[]{:S(2)}, u32[]{:S(2)}) async-start(bf16[4,136,2176]{2,1,0:T(8,128)(2,1)} %bitcast.381), calls=%async_computation.15 | async-start | bytes 4734976 | tf_op jit(solution)/shard_map/all_to_all | solution.py:58
  867.2 42.0 %all-to-all-start.27 = ((bf16[16,136,640]{2,1,0:T(8,128)(2,1)}), bf16[16,136,640]{2,1,0:T(8,128)(2,1)}, u32[]{:S(2)}, u32[]{:S(2)}) async-start(bf16[16,136,640]{2,1,0:T(8,128)(2,1)} %broadcast_in_dim.300), calls=%async_computation.28 | async-start | bytes 5570560 | tf_op jit(solution)/shard_map/all_to_all | solution.py:58
  872.0 162.2 %all-reduce.5.cloned.1.call-start = ((), (), s32[]{:S(2)}) async-start(), calls=%async_computation.35 | async-start | bytes 3551232 | tf_op jit(solution)/shard_map/psum | solution.py:331
  927.6 50.1 %collective-permute-start.26 = (bf16[544,2176]{1,0:T(8,128)(2,1)}, bf16[544,2176]{1,0:T(8,128)(2,1)}, u32[]{:S(2)}, u32[]{:S(2)}) collective-permute-start(bf16[544,2176]{1,0:T(8,128)(2,1)} %pad_maximum_fusion.3), channel_id=1, source_target_pairs={{0,4},{1,5},{2,6},{3,7},{4,64},{5,65},{6,66},{7,67},{8,76},{9,77},... | collective-permute-start | bytes 7102472 | tf_op jit(solution)/shard_map/ppermute | solution.py:54
  1043.5 33.9 %all-to-all-start.22 = ((bf16[4,136,2176]{2,1,0:T(8,128)(2,1)}), bf16[4,136,2176]{2,1,0:T(8,128)(2,1)S(1)}, u32[]{:S(2)}, u32[]{:S(2)}) async-start(bf16[4,136,2176]{2,1,0:T(8,128)(2,1)} %bitcast.91), calls=%async_computation.23 | async-start | bytes 4734976 | tf_op jit(solution)/shard_map/all_to_all | solution.py:58
  (170 other events, 1720.9 us)
Sparse Core Ops, SparseCore 0:
  44.8 76.7 all-gather.3
  123.2 99.5 all-gather.5
  224.4 67.7 all-gather.7
  455.8 68.2 reduce-scatter.9
  562.1 61.8 reduce-scatter.11
  725.7 96.5 reduce-scatter.13
  938.8 95.3 all-reduce.4
